TPU v7x, 128 devices: a whole 4x4x4 slice. The times are simulated.
128 devices in a mesh: grp: 8 (over z, core), blk: 16 (over x, y).
Axes of the slice: x: 4, y: 4, z: 4, core: 2. Of those that a mesh axis runs over, the one named last changes fastest.
Arguments:
- left_tensor: bfloat16 [8, 3072, 768], P('grp', 'blk'), may hold values from -6 to 6
- right_tensor: bfloat16 [8, 768, 3072], P('grp', 'blk'), may hold values from -0.21875 to 0.21875
- diag_gate: float32 [8, 3072], P('grp'), may hold values from 0.2 to 1
- hop_gate: float32 [8, 3072], P('grp'), may hold values from -0.6 to 0.6
- sketch: bfloat16 [3072, 768], replicated, may hold values from -0.109375 to 0.109375
- sector_rows: int32 [8], P('grp'), may hold values from 1536 to 3072, as said below
- kept: int32 [8], P('grp'), may hold values from 384 to 768, as said below
Outputs:
- left_out: float32 [8, 3072, 768], P('grp', 'blk')
- right_out: float32 [3072, 8, 768], P('blk', 'grp')
Inputs may be any that keep to these rules, and one draw needn't show every extreme that they name: `sector_rows`: reached by some sector in every draw, at both ends. `kept`: reached by some sector in every draw, at both ends.
All inputs are finite; a program needn't handle non-finite values.
Results may differ from a plain program's by a relative error of at most 0.022.
Values may be sent and summed in bfloat16 or wider, within the bound.
A program may use at most 128 MiB of HBM per device.

v0:
```python
import math
import jax
import jax.numpy as jnp
from jax import lax
from jax.sharding import PartitionSpec as P


def padded_2(x, sides, width):
    for axis, dim in sides:
        size, length = (lax.axis_size(axis), x.shape[dim])
        up = [(i, (i + 1) % size) for i in range(size - 1)]
        down = [(j, i) for i, j in up]
        last = lax.slice_in_dim(x, length - width, length, axis=dim)
        initial = lax.slice_in_dim(x, 0, width, axis=dim)
        before = lax.ppermute(last, axis, up)
        after = lax.ppermute(initial, axis, down)
        x = jnp.concatenate([before, x, after], axis=dim)
    return x


def body(left_tensor, right_tensor, diag_gate, hop_gate, sketch, sector_rows, kept):
    sectors_here, rows_here, middle_states = left_tensor.shape
    kept_width = sketch.shape[1]
    blk_count = lax.axis_size("blk")
    total_rows = rows_here * blk_count
    theta_full = jnp.einsum(
        "srx,sxc->src",
        left_tensor,
        lax.all_gather(right_tensor, "blk", axis=1, tiled=True),
        preferred_element_type=jnp.float32,
    ).astype(jnp.bfloat16)
    padded = padded_2(theta_full, (("grp", 0),), 1).astype(jnp.float32)
    centre = padded[1:-1]
    mixed_wide = diag_gate[:, None, :] * centre + hop_gate[:, None, :] * (padded[:-2] + padded[2:])
    row_index = lax.axis_index("blk") * rows_here + jnp.arange(rows_here, dtype=jnp.int32)
    row_live = (row_index[None, :] < sector_rows[:, None]).astype(jnp.float32)
    mixed_b = (mixed_wide * row_live[:, :, None]).astype(jnp.bfloat16)
    col_live = (jnp.arange(kept_width, dtype=jnp.int32)[None, :] < kept[:, None]).astype(
        jnp.float32
    )
    sketched = jnp.einsum("src,ck->srk", mixed_b, sketch, preferred_element_type=jnp.float32)
    sketched = (sketched * col_live[:, None, :]).astype(jnp.bfloat16)
    gram_local = jnp.einsum("srk,srj->skj", sketched, sketched, preferred_element_type=jnp.float32)
    gram_mat = lax.psum(gram_local, "blk")
    gram_mat = (
        gram_mat + (1.0 - col_live)[:, :, None] * jnp.eye(kept_width, dtype=jnp.float32)[None]
    )
    factor = jnp.linalg.cholesky(gram_mat)
    sketch_wide = sketched.astype(jnp.float32)
    ortho_basis = lax.linalg.triangular_solve(
        factor, sketch_wide, left_side=False, lower=True, transpose_a=True
    )
    row_scale = math.sqrt(total_rows)
    left_out = ortho_basis * row_scale
    basis_b = ortho_basis.astype(jnp.bfloat16)
    summed = lax.psum_scatter(
        jnp.einsum("src,srk->csk", mixed_b, basis_b, preferred_element_type=jnp.float32).astype(
            jnp.bfloat16
        ),
        "blk",
        scatter_dimension=0,
        tiled=True,
    ).astype(jnp.float32)
    right_out = summed / row_scale
    return (left_out, right_out)


def solution(mesh):
    in_specs = (
        P("grp", "blk", None),
        P("grp", "blk", None),
        P("grp", None),
        P("grp", None),
        P(),
        P("grp"),
        P("grp"),
    )
    out_specs = (P("grp", "blk", None), P("blk", "grp", None))
    return jax.shard_map(body, mesh=mesh, in_specs=in_specs, out_specs=out_specs, check_vma=False)
```

profile of v0, /device:TPU:0, one launch (start us, length us, event | category | flops | bytes accessed | tf_op | source)
XLA Modules:
  0.0 565.9 jit_solution(544307361954773672)
XLA Ops:
  8.0 58.6 %all-gather.2.cloned.1.call-done = bf16[1,768,3072]{2,1,0:T(8,128)(2,1)} async-done(((bf16[1,48,3072]{2,1,0:T(8,128)(2,1)}), bf16[1,768,3072]{2,1,0:T(8,128)(2,1)}) %all-gather.2.cloned.1.call-update) | async-done | bytes 4718608 | tf_op jit(solution)/shard_map/all_gather | solution.py:29
  66.6 3.5 fusion.6
  74.6 3.5 collective-permute-done.1
  84.4 103.3 %all-reduce.3.cloned.1.call-done = f32[1,768,768]{1,2,0:T(8,128)} async-done(((f32[1,768,768]{1,2,0:T(8,128)}), f32[1,768,768]{1,2,0:T(8,128)}) %all-reduce.3.cloned.1.call-update) | async-done | bytes 2359312 | tf_op jit(solution)/shard_map/psum | solution.py:44
  187.7 3.2 select_add_fusion
  190.9 2.2 copy.25
  193.1 2.0 fusion.13
  196.5 11.7 %custom-call.52 = f32[1,128,128]{2,1,0:T(8,128)S(1)} custom-call(f32[1,128,128]{2,1,0:T(8,128)S(1)} %cholesky.424), custom_call_target="Cholesky" | custom-call | tf_op jit(solution)/shard_map/jit(cholesky)/cholesky | solution.py:48
  208.2 9.8 %custom-call.53 = f32[1,1,128,128]{2,3,1,0:T(8,128)S(1)} custom-call(f32[1,1,128,128]{3,2,1,0:T(8,128)S(1)} %get-tuple-element.51), custom_call_target="InvertDiagBlocksLowerTriangular" | custom-call | tf_op jit(solution)/shard_map/jit(cholesky)/cholesky | solution.py:48
  221.2 11.7 %custom-call.54 = f32[1,128,128]{2,1,0:T(8,128)S(1)} custom-call(f32[1,128,128]{2,1,0:T(8,128)S(1)} %cholesky.428), custom_call_target="Cholesky" | custom-call | tf_op jit(solution)/shard_map/jit(cholesky)/cholesky | solution.py:48
  236.0 11.5 %custom-call.55 = f32[1,1,128,128]{2,3,1,0:T(8,128)} custom-call(f32[1,1,128,128]{3,2,1,0:T(8,128)} %get-tuple-element.49), custom_call_target="InvertDiagBlocksLowerTriangular" | custom-call | tf_op jit(solution)/shard_map/jit(cholesky)/cholesky | solution.py:48
  253.0 13.2 %custom-call.56 = f32[1,128,128]{2,1,0:T(8,128)} custom-call(f32[1,128,128]{2,1,0:T(8,128)} %cholesky.433), custom_call_target="Cholesky" | custom-call | tf_op jit(solution)/shard_map/jit(cholesky)/cholesky | solution.py:48
  270.1 11.3 %custom-call.57 = f32[1,1,128,128]{2,3,1,0:T(8,128)} custom-call(f32[1,1,128,128]{3,2,1,0:T(8,128)} %get-tuple-element.47), custom_call_target="InvertDiagBlocksLowerTriangular" | custom-call | tf_op jit(solution)/shard_map/jit(cholesky)/cholesky | solution.py:48
  282.7 2.1 fusion.20
  286.1 13.6 %custom-call.58 = f32[1,128,128]{2,1,0:T(8,128)} custom-call(f32[1,128,128]{2,1,0:T(8,128)} %cholesky.438), custom_call_target="Cholesky" | custom-call | tf_op jit(solution)/shard_map/jit(cholesky)/cholesky | solution.py:48
  303.5 11.3 %custom-call.59 = f32[1,1,128,128]{2,3,1,0:T(8,128)} custom-call(f32[1,1,128,128]{3,2,1,0:T(8,128)} %get-tuple-element.45), custom_call_target="InvertDiagBlocksLowerTriangular" | custom-call | tf_op jit(solution)/shard_map/jit(cholesky)/cholesky | solution.py:48
  319.2 13.2 %custom-call.60 = f32[1,128,128]{2,1,0:T(8,128)} custom-call(f32[1,128,128]{2,1,0:T(8,128)} %cholesky.443), custom_call_target="Cholesky" | custom-call | tf_op jit(solution)/shard_map/jit(cholesky)/cholesky | solution.py:48
  332.4 2.0 select_reduce_fusion.1
  336.8 11.3 %custom-call.61 = f32[1,1,128,128]{2,3,1,0:T(8,128)} custom-call(f32[1,1,128,128]{3,2,1,0:T(8,128)} %get-tuple-element.43), custom_call_target="InvertDiagBlocksLowerTriangular" | custom-call | tf_op jit(solution)/shard_map/jit(cholesky)/cholesky | solution.py:48
  349.2 2.3 fusion.34
  351.5 13.2 %custom-call.62 = f32[1,128,128]{2,1,0:T(8,128)} custom-call(f32[1,128,128]{2,1,0:T(8,128)} %fusion.34), custom_call_target="Cholesky" | custom-call | tf_op jit(solution)/shard_map/jit(cholesky)/cholesky | solution.py:48
  378.5 22.4 %while.1 = (s32[]{:T(128)}, f32[1,768,768]{1,2,0:T(8,128)}, s32[6,2]{0,1:T(2,128)S(1)}, f32[6,1,128,128]{3,2,1,0:T(8,128)}, s32[]{:T(128)}) while((s32[]{:T(128)}, f32[1,768,768]{1,2,0:T(8,128)}, s32[6,2]{0,1:T(2,128)S(1)}, f32[6,1,128,128]{3,2,1,0:T(8,128)}, s32[]{:T(128)}) %tuple.47), condition=%wide.while_cond, body=%wide.while_body.sunk | while | flops 2 | bytes 393833 | solution.py:50
  379.2 2.3 constant_dynamic-slice_fusion.5
  382.9 2.3 constant_dynamic-slice_fusion.5
  386.7 2.3 constant_dynamic-slice_fusion.5
  390.4 2.3 constant_dynamic-slice_fusion.5
  394.1 2.3 constant_dynamic-slice_fusion.5
  397.9 2.3 constant_dynamic-slice_fusion.5
  400.9 59.8 %custom-call.63 = f32[1,6,128,128]{2,3,1,0:T(8,128)S(1)} custom-call(f32[1,6,128,128]{3,2,1,0:T(8,128)} %bitcast.298), custom_call_target="InvertDiagBlocksLowerTriangular" | custom-call | tf_op jit(solution)/shard_map/triangular_solve | solution.py:50
  468.9 3.6 fusion.2
  472.5 6.6 %copy.46 = bf16[3072,768]{1,0:T(8,128)(2,1)} copy(bf16[3072,768]{0,1:T(8,128)(2,1)} %fusion.2) | data formatting | bytes 9437184
  480.0 76.8 %reduce-scatter.4.cloned.1.call-done = bf16[192,768]{1,0:T(8,128)(2,1)} async-done(((bf16[3072,768]{1,0:T(8,128)(2,1)}), bf16[192,768]{1,0:T(8,128)(2,1)}) %reduce-scatter.4.cloned.1.call-update) | async-done | bytes 294928
  (133 shorter events, 71.4 us)
Async XLA Ops:
  7.2 59.4 %copy-start = (bf16[1,192,768]{2,1,0:T(8,128)(2,1)S(1)}, bf16[1,192,768]{2,1,0:T(8,128)(2,1)}, u32[]{:S(2)}) copy-start(bf16[1,192,768]{2,1,0:T(8,128)(2,1)} %param.7) | copy-start | bytes 884740
  7.2 59.4 %all-gather.2.cloned.1.call-start = ((), (), s32[]{:S(2)}) async-start(), calls=%async_computation.1 | async-start | bytes 5013504 | tf_op jit(solution)/shard_map/all_gather | solution.py:29
  7.9 179.7 %all-reduce.3.cloned.1.call-start = ((), (), s32[]{:S(2)}) async-start(), calls=%async_computation.2 | async-start | bytes 4718592 | tf_op jit(solution)/shard_map/psum | solution.py:44
  66.6 14.1 %slice-start = ((s8[4718592]{0:T(1024)(128)(4,1)}), s8[524288]{0:T(1024)(128)(4,1)S(1)}, s32[]{:S(2)}) async-start(s8[4718592]{0:T(1024)(128)(4,1)} %bitcast.283), calls=%async_computation.4 | async-start | bytes 1048576
  70.1 4.5 collective-permute-start
  71.9 6.1 %collective-permute-start.1 = (bf16[1,192,3072]{2,1,0:T(8,128)(2,1)S(1)}, bf16[1,192,3072]{2,1,0:T(8,128)(2,1)}, u32[]{:S(2)}, u32[]{:S(2)}) collective-permute-start(bf16[1,192,3072]{2,1,0:T(8,128)(2,1)S(1)} %fusion.6), channel_id=1, source_target_pairs={{16,0},{32,16},{48,32},{64,48},{80,64},{96,80},{112,96},{17,1},{33... | collective-permute-start | bytes 3538952 | tf_op jit(solution)/shard_map/ppermute | solution.py:16
  74.5 5.3 copy-start.10
  74.5 5.3 copy-start.11
  74.5 6.2 %slice-start.1 = ((s8[4718592]{0:T(1024)(128)(4,1)}), s8[4194304]{0:T(1024)(128)(4,1)S(1)}, s32[]{:S(2)}) async-start(s8[4718592]{0:T(1024)(128)(4,1)} %bitcast.283), calls=%async_computation.5 | async-start | bytes 8388608
  80.7 1.1 copy-start.1
  83.8 473.0 %reduce-scatter.4.cloned.1.call-start = ((), (), s32[]{:S(2)}) async-start(), calls=%async_computation.3 | async-start | bytes 5013504
  195.1 1.4 copy-start.3
  219.6 14.6 %copy-start.4 = (f32[640,128]{0,1:T(8,128)}, f32[640,128]{0,1:T(8,128)S(1)}, u32[]{:S(2)}) copy-start(f32[640,128]{0,1:T(8,128)S(1)} %copy.26) | copy-start | bytes 983044
  221.1 13.1 %copy-start.6 = (f32[1,640,128]{2,1,0:T(8,128)}, f32[1,640,128]{2,1,0:T(8,128)S(1)}, u32[]{:S(2)}) copy-start(f32[1,640,128]{2,1,0:T(8,128)S(1)} %fusion.16) | copy-start | bytes 983044
  235.0 1.0 copy-start.5
  251.7 0.7 copy-start.7
  284.8 0.7 copy-start.8
  317.9 0.7 copy-start.9
  376.9 1.6 copy-start.12
  463.5 5.5 copy-start.2
Sparse Core Ops, SparseCore 0:
  10.2 56.3 all-gather.1
  83.9 103.6 all-reduce.2
  479.3 77.5 reduce-scatter.3
where the time goes:
time: 572 us; the launch traced here: 566 us
  waiting for transfers between devices  243 us (42%)
  other arithmetic  214 us (37%)
  local copies, waits for them, and re-layouts  51.9 us (9%)
  matrix products  34.4 us (6%)
  between operations  19.5 us (3%)
    another operation x22, other arithmetic, body(): factor = jnp.linalg.cholesky(gram_mat)  143 us
    psum x1, waiting for transfers between devices, body(): gram_mat = lax.psum(gram_local, 'blk')  103 us
    unnamed x4, waiting for transfers between devices  77.5 us
    another operation x3, other arithmetic, body(): lax.linalg.triangular_solve(factor, sketch_wide, left_side=False, lower=T...  61.9 us
    all_gather x1, waiting for transfers between devices, body(): lax.all_gather(right_tensor, 'blk', axis=1, tiled=True)  58.6 us
    another operation x30, local copies, waits for them, and re-layouts  22.3 us
    another operation x10, matrix products, body(): factor = jnp.linalg.cholesky(gram_mat)  16.2 us
    another operation x19, local copies, waits for them, and re-layouts, body(): factor = jnp.linalg.cholesky(gram_mat)  15 us
  transfers between devices with their start and end apart: 5, of which 4 were waited for; matrix products, arithmetic and copies ran while one was open for 0% of the time, Pallas kernels for 0%

commit v1 on v0

--- a/solution.py
+++ b/solution.py
@@ -41,7 +41,7 @@
     sketched = jnp.einsum("src,ck->srk", mixed_b, sketch, preferred_element_type=jnp.float32)
     sketched = (sketched * col_live[:, None, :]).astype(jnp.bfloat16)
     gram_local = jnp.einsum("srk,srj->skj", sketched, sketched, preferred_element_type=jnp.float32)
-    gram_mat = lax.psum(gram_local, "blk")
+    gram_mat = jnp.sum(lax.all_gather(gram_local, "blk"), axis=0)
     gram_mat = (
         gram_mat + (1.0 - col_live)[:, :, None] * jnp.eye(kept_width, dtype=jnp.float32)[None]
     )

time: 572 us -> 690 us (1.21)
  waiting for transfers between devices: 243 us -> 371 us
  local copies, waits for them, and re-layouts: 51.9 us -> 43.5 us
    all_gather x0 -> x1, waiting for transfers between devices: none -> 231 us  [body(): gram_mat = jnp.sum(lax.all_gather(gram_local, 'blk'), axis=0)]
    psum x1 -> x0, waiting for transfers between devices: 103 us -> none  [body(): gram_mat = lax.psum(gram_local, 'blk')]
    reduce_sum x0 -> x1, other arithmetic: none -> 15.1 us  [body(): gram_mat = jnp.sum(lax.all_gather(gram_local, 'blk'), axis=0)]
    another operation x22, other arithmetic: 143 us -> 132 us  [body(): factor = jnp.linalg.cholesky(gram_mat)]
    another operation x19, local copies, waits for them, and re-layouts: 15 us -> 5.99 us  [body(): factor = jnp.linalg.cholesky(gram_mat)]
where the time goes in v1:
time: 690 us; the launch traced here: 684 us
  waiting for transfers between devices  371 us (54%)
  other arithmetic  215 us (31%)
  local copies, waits for them, and re-layouts  43.5 us (6%)
  matrix products  31.9 us (5%)
  between operations  19.6 us (3%)
    all_gather x1, waiting for transfers between devices, body(): gram_mat = jnp.sum(lax.all_gather(gram_local, 'blk'), axis=0)  231 us
    another operation x22, other arithmetic, body(): factor = jnp.linalg.cholesky(gram_mat)  132 us
    unnamed x4, waiting for transfers between devices  78.1 us
    another operation x3, other arithmetic, body(): lax.linalg.triangular_solve(factor, sketch_wide, left_side=False, lower=T...  61.3 us
    all_gather x1, waiting for transfers between devices, body(): lax.all_gather(right_tensor, 'blk', axis=1, tiled=True)  58.6 us
    another operation x30, local copies, waits for them, and re-layouts  21.1 us
    reduce_sum x1, other arithmetic, body(): gram_mat = jnp.sum(lax.all_gather(gram_local, 'blk'), axis=0)  15.1 us
  transfers between devices with their start and end apart: 5, of which 4 were waited for; matrix products, arithmetic and copies ran while one was open for 0% of the time, Pallas kernels for 0%

profile of v1, /device:TPU:0, one launch (start us, length us, event | category | flops | bytes accessed | tf_op | source)
XLA Modules:
  0.0 684.4 jit_solution(17125785260043376109)
XLA Ops:
  8.0 58.6 %all-gather.4.cloned.1.call-done = bf16[1,768,3072]{2,1,0:T(8,128)(2,1)} async-done(((bf16[1,48,3072]{2,1,0:T(8,128)(2,1)}), bf16[1,768,3072]{2,1,0:T(8,128)(2,1)}) %all-gather.4.cloned.1.call-update) | async-done | bytes 4718608 | tf_op jit(solution)/shard_map/all_gather | solution.py:29
  66.6 3.5 fusion.6
  74.6 3.5 collective-permute-done.1
  83.9 230.8 %all-gather.6.cloned.1.call-done = f32[12288,768]{1,0:T(8,128)} async-done(((f32[768,768]{1,0:T(8,128)}), f32[12288,768]{1,0:T(8,128)}) %all-gather.6.cloned.1.call-update) | async-done | bytes 37748752 | tf_op jit(solution)/shard_map/all_gather | solution.py:44
  314.7 15.1 %reduce.55 = f32[768,768]{1,0:T(8,128)} reduce(f32[16,768,768]{2,1,0:T(8,128)} %bitcast.286, f32[]{:T(128)} %constant.244.clone.1), dimensions={0}, to_apply=%region_0.0 | reduce | flops 8847360 | bytes 40108036 | tf_op jit(solution)/shard_map/reduce_sum | solution.py:44
  329.8 2.0 copy.23
  333.4 3.2 copy.24
  336.6 2.0 fusion.13
  340.0 11.7 %custom-call.52 = f32[1,128,128]{2,1,0:T(8,128)S(1)} custom-call(f32[1,128,128]{2,1,0:T(8,128)S(1)} %cholesky.424), custom_call_target="Cholesky" | custom-call | tf_op jit(solution)/shard_map/jit(cholesky)/cholesky | solution.py:48
  351.7 9.8 %custom-call.53 = f32[1,1,128,128]{2,3,1,0:T(8,128)S(1)} custom-call(f32[1,1,128,128]{3,2,1,0:T(8,128)S(1)} %get-tuple-element.51), custom_call_target="InvertDiagBlocksLowerTriangular" | custom-call | tf_op jit(solution)/shard_map/jit(cholesky)/cholesky | solution.py:48
  364.6 11.7 %custom-call.54 = f32[1,128,128]{2,1,0:T(8,128)S(1)} custom-call(f32[1,128,128]{2,1,0:T(8,128)S(1)} %cholesky.428), custom_call_target="Cholesky" | custom-call | tf_op jit(solution)/shard_map/jit(cholesky)/cholesky | solution.py:48
  377.6 10.0 %custom-call.55 = f32[1,1,128,128]{2,3,1,0:T(8,128)S(1)} custom-call(f32[1,1,128,128]{3,2,1,0:T(8,128)S(1)} %get-tuple-element.49), custom_call_target="InvertDiagBlocksLowerTriangular" | custom-call | tf_op jit(solution)/shard_map/jit(cholesky)/cholesky | solution.py:48
  389.0 1.9 fusion.18
  391.6 13.2 %custom-call.56 = f32[1,128,128]{2,1,0:T(8,128)} custom-call(f32[1,128,128]{2,1,0:T(8,128)} %cholesky.433), custom_call_target="Cholesky" | custom-call | tf_op jit(solution)/shard_map/jit(cholesky)/cholesky | solution.py:48
  408.6 11.3 %custom-call.57 = f32[1,1,128,128]{2,3,1,0:T(8,128)} custom-call(f32[1,1,128,128]{3,2,1,0:T(8,128)} %get-tuple-element.47), custom_call_target="InvertDiagBlocksLowerTriangular" | custom-call | tf_op jit(solution)/shard_map/jit(cholesky)/cholesky | solution.py:48
  421.2 2.1 fusion.20
  423.9 12.9 %custom-call.58 = f32[1,128,128]{2,1,0:T(8,128)S(1)} custom-call(f32[1,128,128]{2,1,0:T(8,128)} %cholesky.438), custom_call_target="Cholesky" | custom-call | tf_op jit(solution)/shard_map/jit(cholesky)/cholesky | solution.py:48
  439.0 10.6 %custom-call.59 = f32[1,1,128,128]{2,3,1,0:T(8,128)S(1)} custom-call(f32[1,1,128,128]{3,2,1,0:T(8,128)} %get-tuple-element.45), custom_call_target="InvertDiagBlocksLowerTriangular" | custom-call | tf_op jit(solution)/shard_map/jit(cholesky)/cholesky | solution.py:48
  451.9 11.7 %custom-call.60 = f32[1,128,128]{2,1,0:T(8,128)S(1)} custom-call(f32[1,128,128]{2,1,0:T(8,128)S(1)} %cholesky.443), custom_call_target="Cholesky" | custom-call | tf_op jit(solution)/shard_map/jit(cholesky)/cholesky | solution.py:48
  464.4 10.6 %custom-call.61 = f32[1,1,128,128]{2,3,1,0:T(8,128)S(1)} custom-call(f32[1,1,128,128]{3,2,1,0:T(8,128)} %get-tuple-element.43), custom_call_target="InvertDiagBlocksLowerTriangular" | custom-call | tf_op jit(solution)/shard_map/jit(cholesky)/cholesky | solution.py:48
  477.1 11.7 %custom-call.62 = f32[1,128,128]{2,1,0:T(8,128)S(1)} custom-call(f32[1,128,128]{2,1,0:T(8,128)S(1)} %fusion.34), custom_call_target="Cholesky" | custom-call | tf_op jit(solution)/shard_map/jit(cholesky)/cholesky | solution.py:48
  497.7 21.2 %while.1 = (s32[]{:T(128)}, f32[1,768,768]{1,2,0:T(8,128)}, s32[6,2]{0,1:T(2,128)S(1)}, f32[6,1,128,128]{3,2,1,0:T(8,128)}, s32[]{:T(128)}) while((s32[]{:T(128)}, f32[1,768,768]{1,2,0:T(8,128)}, s32[6,2]{0,1:T(2,128)S(1)}, f32[6,1,128,128]{3,2,1,0:T(8,128)}, s32[]{:T(128)}) %tuple.47), condition=%wide.while_cond, body=%wide.while_body.sunk | while | flops 2 | bytes 393833 | solution.py:50
  498.2 2.2 constant_dynamic-slice_fusion.5
  501.8 2.2 constant_dynamic-slice_fusion.5
  505.3 2.2 constant_dynamic-slice_fusion.5
  508.9 2.2 constant_dynamic-slice_fusion.5
  512.4 2.2 constant_dynamic-slice_fusion.5
  515.9 2.1 constant_dynamic-slice_fusion.5
  518.8 59.8 %custom-call.63 = f32[1,6,128,128]{2,3,1,0:T(8,128)S(1)} custom-call(f32[1,6,128,128]{3,2,1,0:T(8,128)} %bitcast.302), custom_call_target="InvertDiagBlocksLowerTriangular" | custom-call | tf_op jit(solution)/shard_map/triangular_solve | solution.py:50
  586.9 3.6 fusion.2
  590.5 6.6 copy.44
  598.0 77.3 %reduce-scatter.4.cloned.1.call-done = bf16[192,768]{1,0:T(8,128)(2,1)} async-done(((bf16[3072,768]{1,0:T(8,128)(2,1)}), bf16[192,768]{1,0:T(8,128)(2,1)}) %reduce-scatter.4.cloned.1.call-update) | async-done | bytes 294928
  (129 shorter events, 56.3 us)
Async XLA Ops:
  7.2 59.4 %copy-start = (bf16[1,192,768]{2,1,0:T(8,128)(2,1)S(1)}, bf16[1,192,768]{2,1,0:T(8,128)(2,1)}, u32[]{:S(2)}) copy-start(bf16[1,192,768]{2,1,0:T(8,128)(2,1)} %param.7) | copy-start | bytes 884740
  7.2 59.4 %all-gather.4.cloned.1.call-start = ((), (), s32[]{:S(2)}) async-start(), calls=%async_computation.1 | async-start | bytes 5013504 | tf_op jit(solution)/shard_map/all_gather | solution.py:29
  7.9 306.7 %all-gather.6.cloned.1.call-start = ((), (), s32[]{:S(2)}) async-start(), calls=%async_computation.2 | async-start | bytes 40108032 | tf_op jit(solution)/shard_map/all_gather | solution.py:44
  66.6 14.1 %slice-start = ((s8[4718592]{0:T(1024)(128)(4,1)}), s8[524288]{0:T(1024)(128)(4,1)S(1)}, s32[]{:S(2)}) async-start(s8[4718592]{0:T(1024)(128)(4,1)} %bitcast.287), calls=%async_computation.4 | async-start | bytes 1048576
  70.1 4.5 collective-permute-start
  71.9 6.1 collective-permute-start.1
  74.5 5.3 copy-start.8
  74.5 5.3 copy-start.9
  74.6 6.2 slice-start.1
  80.7 1.1 copy-start.2
  83.8 591.5 %reduce-scatter.4.cloned.1.call-start = ((), (), s32[]{:S(2)}) async-start(), calls=%async_computation.3 | async-start | bytes 5013504
  338.6 1.4 copy-start.4
  363.1 13.4 %copy-start.5 = (f32[640,128]{0,1:T(8,128)}, f32[640,128]{0,1:T(8,128)S(1)}, u32[]{:S(2)}) copy-start(f32[640,128]{0,1:T(8,128)S(1)} %copy.25) | copy-start | bytes 983044
  364.6 11.9 %copy-start.7 = (f32[1,640,128]{2,1,0:T(8,128)}, f32[1,640,128]{2,1,0:T(8,128)S(1)}, u32[]{:S(2)}) copy-start(f32[1,640,128]{2,1,0:T(8,128)S(1)} %fusion.16) | copy-start | bytes 983044
  376.6 1.0 copy-start.6
  581.4 5.5 copy-start.3
  597.1 80.6 %copy-start.1 = (bf16[1,192,768]{2,1,0:T(8,128)(2,1)S(1)}, bf16[1,192,768]{2,1,0:T(8,128)(2,1)}, u32[]{:S(2)}) copy-start(bf16[1,192,768]{2,1,0:T(8,128)(2,1)} %param.7) | copy-start | bytes 884740
Sparse Core Ops, SparseCore 0:
  10.2 56.3 all-gather.3
  83.9 230.6 all-gather.5
  597.2 78.0 reduce-scatter.3
